TPU v7x, 32 devices: a whole 2x2x4 slice. The times are simulated.
32 devices in a mesh: seq: 8 (over y, x, core), chan: 4 (over z).
Axes of the slice: x: 2, y: 2, z: 4, core: 2. Of those that a mesh axis runs over, the one named last changes fastest.
Arguments:
- tokens: bfloat16 [2048, 512], P('seq', 'chan'), may hold values from -6 to 6
- in_weight: bfloat16 [3, 512, 512], P(None, None, 'chan'), may hold values from -0.25 to 0.25
- out_weight: bfloat16 [512, 512], P(None, 'chan'), may hold values from -0.25 to 0.25
- decay_rates: float32 [16, 512], P(None, 'chan'), may hold values from 0.00048828125 to 0.03
- residues: float32 [16, 512], P(None, 'chan'), may hold values from -1.8 to 1.8
- skip_gain: float32 [512], P('chan'), may hold values from -5 to 5
Outputs:
- block_out: bfloat16 [2048, 512], P('seq', 'chan')
All inputs are finite; a program needn't handle non-finite values.
Results may differ from a plain program's by a relative error of at most 0.013.
Values may be sent and summed in bfloat16 or wider, within the bound.
A program may use at most 64 MiB of HBM per device.

v0:
```python
import math

import jax
import jax.numpy as jnp
from jax import lax
from jax.sharding import PartitionSpec as P

highest = lax.Precision.HIGHEST


def for_sending(shard):
    return jax.tree.map(lambda a: a.astype(jnp.bfloat16) if a.dtype == jnp.float32 else a, shard)


def angle_table(row_index, col_index, modulus, sign):
    product_index = row_index[:, None] * col_index[None, :] % modulus
    turn = product_index.astype(jnp.float32) * (sign * 2.0 * math.pi / modulus)
    return (jnp.cos(turn), jnp.sin(turn))


def fold_channels(activations, adder, initial):
    return adder(initial, lax.all_gather(activations, "chan", axis=1, tiled=True), jnp.int32(0))


def forward_outer(signal, outer, total):
    row_count, column_count, chan_count = signal.shape
    cos_table, sin_table = angle_table(
        jnp.arange(outer, dtype=jnp.int32), jnp.arange(row_count, dtype=jnp.int32), outer, -1.0
    )
    flat = signal.reshape(row_count, column_count * chan_count)
    real_part = jnp.dot(cos_table, flat, precision=highest).reshape(outer, column_count, chan_count)
    imag_part = jnp.dot(sin_table, flat, precision=highest).reshape(outer, column_count, chan_count)
    columns = jnp.arange(column_count, dtype=jnp.int32)
    twist_real, twist_imag = angle_table(jnp.arange(outer, dtype=jnp.int32), columns, total, -1.0)
    twist_real = twist_real[:, :, None]
    twist_imag = twist_imag[:, :, None]
    return (
        real_part * twist_real - imag_part * twist_imag,
        real_part * twist_imag + imag_part * twist_real,
    )


def filter_spectrum(freqs, decay_rates, residues, total):
    half_length = total // 2
    phase = freqs.astype(jnp.float32)[:, :, None] * (2.0 * math.pi / total)
    half_sine = jnp.sin(0.5 * phase)
    full_sine = jnp.sin(phase)
    parity = (1 - 2 * (freqs % 2)).astype(jnp.float32)[:, :, None]
    spec_real = jnp.zeros(freqs.shape + (decay_rates.shape[1],), jnp.float32)
    spec_imag = jnp.zeros(freqs.shape + (decay_rates.shape[1],), jnp.float32)
    for mode_index in range(decay_rates.shape[0]):
        rate = decay_rates[mode_index][None, None, :]
        decay = jnp.exp(-rate)
        lead = -jnp.expm1(-rate) + decay * 2.0 * half_sine * half_sine
        cross = decay * full_sine
        numerator = 1.0 - parity * jnp.exp(-rate * half_length)
        factor = (
            residues[mode_index][None, None, :]
            * jnp.sqrt(2.0 * rate)
            * numerator
            / (lead * lead + cross * cross)
        )
        spec_real = spec_real + factor * lead
        spec_imag = spec_imag - factor * cross
    return (spec_real, spec_imag)


def middle_pass(real_part, imag_part, outer, decay_rates, residues, total):
    outer_count, inner, chan_count = real_part.shape
    inner_index = jnp.arange(inner, dtype=jnp.int32)
    dft_real, dft_imag = angle_table(inner_index, inner_index, inner, -1.0)
    spec_a = jnp.einsum("qb,kbc->kqc", dft_real, real_part, precision=highest) - jnp.einsum(
        "qb,kbc->kqc", dft_imag, imag_part, precision=highest
    )
    spec_b = jnp.einsum("qb,kbc->kqc", dft_real, imag_part, precision=highest) + jnp.einsum(
        "qb,kbc->kqc", dft_imag, real_part, precision=highest
    )
    outer_index = jnp.arange(outer_count, dtype=jnp.int32)
    freqs = outer_index[:, None] + outer * inner_index[None, :]
    gain_real, gain_imag = filter_spectrum(freqs, decay_rates, residues, total)
    prod_real = spec_a * gain_real - spec_b * gain_imag
    prod_imag = spec_a * gain_imag + spec_b * gain_real
    back_real = jnp.einsum("qb,kqc->kbc", dft_real, prod_real, precision=highest) + jnp.einsum(
        "qb,kqc->kbc", dft_imag, prod_imag, precision=highest
    )
    back_imag = jnp.einsum("qb,kqc->kbc", dft_real, prod_imag, precision=highest) - jnp.einsum(
        "qb,kqc->kbc", dft_imag, prod_real, precision=highest
    )
    twist_real, twist_imag = angle_table(outer_index, inner_index, total, 1.0)
    twist_real = twist_real[:, :, None]
    twist_imag = twist_imag[:, :, None]
    return (
        back_real * twist_real - back_imag * twist_imag,
        back_real * twist_imag + back_imag * twist_real,
    )


def inverse_outer(real_part, imag_part, rows_kept, total):
    outer, column_count, chan_count = real_part.shape
    cos_table, sin_table = angle_table(
        jnp.arange(rows_kept, dtype=jnp.int32), jnp.arange(outer, dtype=jnp.int32), outer, 1.0
    )
    flat_real = real_part.reshape(outer, column_count * chan_count)
    flat_imag = imag_part.reshape(outer, column_count * chan_count)
    result = jnp.dot(cos_table, flat_real, precision=highest) - jnp.dot(
        sin_table, flat_imag, precision=highest
    )
    return (result * (1.0 / total)).reshape(rows_kept, column_count, chan_count)


def on_device(tokens, in_weight, out_weight, decay_rates, residues, skip_gain):
    seq_count = lax.axis_size("seq")
    seq_place = lax.axis_index("seq")
    tok_count, local_chan = tokens.shape
    outer = 2 * seq_count
    total = outer * tok_count

    def add_input(carry, piece, first_index):
        return jnp.einsum("tr,irc->itc", piece, in_weight, preferred_element_type=jnp.float32)

    projected = fold_channels(
        tokens, add_input, jnp.zeros((3, tok_count, local_chan), jnp.float32)
    ).astype(jnp.bfloat16)
    query = projected[0].astype(jnp.float32)
    product = projected[1].astype(jnp.float32) * projected[2].astype(jnp.float32)
    group = local_chan // seq_count
    gathered = lax.all_to_all(
        product.T.astype(jnp.bfloat16), "seq", split_axis=0, concat_axis=1, tiled=True
    ).astype(jnp.float32)
    whole = gathered.reshape(group, seq_count, tok_count).transpose(1, 2, 0)
    rates_mine = lax.dynamic_slice_in_dim(decay_rates, seq_place * group, group, 1)
    weights_mine = lax.dynamic_slice_in_dim(residues, seq_place * group, group, 1)
    real_part, imag_part = forward_outer(whole, outer, total)
    real_part, imag_part = middle_pass(real_part, imag_part, outer, rates_mine, weights_mine, total)
    result = inverse_outer(real_part, imag_part, seq_count, total)
    flat_result = result.transpose(2, 0, 1).reshape(group, seq_count * tok_count)
    convolved = (
        lax.all_to_all(for_sending(flat_result), "seq", split_axis=1, concat_axis=0, tiled=True)
        .astype(flat_result.dtype)
        .T
    )
    mixed = (query * (convolved + skip_gain[None, :] * product)).astype(jnp.bfloat16)

    def add_output(carry, piece, first_index):
        return jnp.dot(piece, out_weight, preferred_element_type=jnp.float32)

    block_out = fold_channels(mixed, add_output, jnp.zeros((tok_count, local_chan), jnp.float32))
    return block_out.astype(jnp.bfloat16)


def solution(mesh):
    return jax.shard_map(
        on_device,
        mesh=mesh,
        in_specs=(
            P("seq", "chan"),
            P(None, None, "chan"),
            P(None, "chan"),
            P(None, "chan"),
            P(None, "chan"),
            P("chan"),
        ),
        out_specs=P("seq", "chan"),
        check_vma=False,
    )
```

profile of v0, /device:TPU:0, one launch (start us, length us, event | category | flops | bytes accessed | tf_op | source)
XLA Modules:
  0.0 68.6 jit_solution(2654546079101123360)
XLA Ops:
  0.0 0.0 copy-start
  0.0 14.8 %all_gather.6 = bf16[256,512]{1,0:T(8,128)(2,1)S(1)} all-gather(bf16[256,128]{1,0:T(8,128)(2,1)} %param.6), channel_id=1, replica_groups=mesh['seq'=8,'chan'=4] {'chan'}, dimensions={1}, use_global_device_ids=true | all-gather | bytes 327680 | tf_op jit(solution)/shard_map/all_gather | solution.py:22
  14.8 0.0 copy-done
  14.8 0.3 fusion.4
  15.1 0.6 bitcast_convert_fusion
  15.8 3.7 %all-to-all-start = ((bf16[8,16,256]{2,1,0:T(8,128)(2,1)}), bf16[8,16,256]{2,1,0:T(8,128)(2,1)S(1)}, u32[]{:S(2)}, u32[]{:S(2)}) async-start(bf16[8,16,256]{2,1,0:T(8,128)(2,1)} %bitcast.6), calls=%async_computation | async-start | bytes 131072 | tf_op jit(solution)/shard_map/all_to_all | solution.py:127
  19.5 1.3 %exponential_bitcast_fusion.31 = (f32[16]{0:T(128)S(1)}, f32[1,16]{1,0:T(1,128)S(1)}, f32[16]{0:T(128)S(1)}, f32[1,16]{1,0:T(1,128)S(1)}, f32[16]{0:T(128)S(1)},...) fusion(f32[16,128]{1,0:T(8,128)} %param.9, ...), kind=kLoop, calls=%fused_computation.282 | loop fusion | flops 544 | bytes 4224 | tf_op jit(solution)/shard_map/exp | solution.py:56
  21.1 0.1 multiply_sine_fusion.1
  21.3 0.1 multiply_sine_fusion.3
  21.4 0.1 multiply_sine_fusion.2
  21.4 3.1 %all-to-all-done = bf16[8,16,256]{2,1,0:T(8,128)(2,1)S(1)} async-done(((bf16[8,16,256]{2,1,0:T(8,128)(2,1)}), bf16[8,16,256]{2,1,0:T(8,128)(2,1)S(1)}, u32[]{:S(2)}, u32[]{:S(2)}) %all-to-all-start) | async-done | bytes 65568 | tf_op jit(solution)/shard_map/all_to_all | solution.py:127
  24.5 0.3 copy.25
  24.8 0.8 %reshape.1050 = bf16[8,4096]{1,0:T(8,128)(2,1)S(1)} reshape(bf16[8,256,16]{2,1,0:T(8,128)(2,1)S(1)} %copy.25) | data formatting | bytes 131072 | tf_op jit(solution)/shard_map/reshape | solution.py:30
  25.5 0.4 dot_general.48
  25.9 0.2 copy.26
  26.2 0.4 fusion.108
  26.5 0.4 multiply_subtract_fusion.1
  26.9 1.5 %fusion.66 = f32[16,16,256]{2,1,0:T(8,128)S(1)} fusion(f32[16,256,16]{1,0,2:T(8,128)S(1)} %get-tuple-element.42), kind=kOutput, calls=%fused_computation.108 | convolution fusion | flops 202244096 | bytes 524288 | tf_op jit(solution)/shard_map/qb,kbc->kqc/dot_general | solution.py:72
  28.4 1.5 %fusion.64 = f32[16,16,256]{2,1,0:T(8,128)S(1)} fusion(f32[16,256,16]{1,0,2:T(8,128)S(1)} %get-tuple-element.43), kind=kOutput, calls=%fused_computation.106 | convolution fusion | flops 202244096 | bytes 524288 | tf_op jit(solution)/shard_map/qb,kbc->kqc/dot_general | solution.py:75
  29.9 1.5 %fusion.3 = f32[16,256,16]{1,2,0:T(8,128)S(1)} fusion(f32[16,16,256]{2,1,0:T(8,128)S(1)} %fusion.66, f32[16,256,16]{1,0,2:T(8,128)S(1)} %get-tuple-element.43), kind=kOutput, calls=%fused_computation.9 | convolution fusion | flops 202309632 | bytes 786432 | tf_op jit(solution)/shard_map/qb,kbc->kqc/dot_general | solution.py:72
  31.3 3.5 %multiply_subtract_fusion = (f32[16,256,16]{1,2,0:T(8,128)S(1)}, f32[16,256,16]{1,2,0:T(8,128)S(1)}, f32[16,256,16]{1,2,0:T(8,128)S(1)}, f32[16,256,16]{1,2,0:T(8,128)S(1)}) fusion(f32[16,256,16]{1,2,0:T(8,128)S(1)} %fusion.3, f32[16]{0:T(128)S(1)} %get-tuple-element.153, f32[16]{0:T(128)S(1)} %get-tuple-element.180, f32[16]{0:T(128)S(1)} %get-tuple-element.152, ...), kind=kOutput, calls=%fused_computation.114 | convolution fusion | flops 218169344 | bytes 1889280 | tf_op jit(solution)/shard_map/qb,kbc->kqc/dot_general | solution.py:75
  34.9 0.1 multiply_add_fusion
  35.0 1.5 %fusion.60 = f32[16,16,256]{2,1,0:T(8,128)S(1)} fusion(f32[16,256,16]{1,2,0:T(8,128)S(1)} %multiply_add_fusion), kind=kOutput, calls=%fused_computation.102 | convolution fusion | flops 202244096 | bytes 524288 | tf_op jit(solution)/shard_map/qb,kqc->kbc/dot_general | solution.py:86
  36.5 1.4 %fusion.62 = f32[16,16,256]{2,1,0:T(8,128)S(1)} fusion(f32[16,256,16]{1,2,0:T(8,128)S(1)} %get-tuple-element.5), kind=kOutput, calls=%fused_computation.104 | convolution fusion | flops 202244096 | bytes 524288 | tf_op jit(solution)/shard_map/qb,kqc->kbc/dot_general | solution.py:83
  37.9 1.4 %convolution_subtract_fusion.1 = f32[16,16,256]{2,1,0:T(8,128)S(1)} fusion(f32[16,16,256]{2,1,0:T(8,128)S(1)} %fusion.60, f32[16,256,16]{1,2,0:T(8,128)S(1)} %get-tuple-element.5), kind=kOutput, calls=%fused_computation.4 | convolution fusion | flops 202309632 | bytes 786432 | tf_op jit(solution)/shard_map/qb,kqc->kbc/dot_general | solution.py:86
  39.2 1.4 %add_bitcast_fusion = (f32[16,256,16]{1,2,0:T(8,128)S(1)}, f32[16,256,16]{1,2,0:T(8,128)S(1)}) fusion(f32[16,16,256]{2,1,0:T(8,128)S(1)} %convolution_subtract_fusion.1, f32[16,256]{1,0:T(8,128)S(1)} %get-tuple-element.196, f32[16,256]{1,0:T(8,128)S(1)} %get-tuple-element.197, f32[16,16,256]{2,1,0:T(8,128)S(1)} %fusion.62, ...), kind=kOutput, calls=%fused_computation.111 | convolution fusion | flops 202702848 | bytes 1343488 | tf_op jit(solution)/shard_map/qb,kqc->kbc/dot_general | solution.py:83
  40.6 0.6 copy.33
  41.2 1.6 %reshape.1052 = f32[16,4096]{1,0:T(8,128)S(1)} reshape(f32[16,256,16]{2,1,0:T(8,128)S(1)} %copy.33) | data formatting | bytes 524288 | tf_op jit(solution)/shard_map/reshape | solution.py:104
  42.8 0.6 copy.32
  43.4 0.0 copy-start.2
  43.4 0.0 copy-start.1
  43.4 1.6 %reshape.1051 = f32[16,4096]{1,0:T(8,128)S(1)} reshape(f32[16,256,16]{2,1,0:T(8,128)S(1)} %copy.32) | data formatting | bytes 524288 | tf_op jit(solution)/shard_map/reshape | solution.py:103
  45.0 0.3 fusion.115
  45.3 0.3 fusion.1
  45.6 0.4 convert_element_type.264
  46.0 0.2 copy.34
  46.2 7.4 %all_to_all.23 = bf16[16,8,256]{2,0,1:T(8,128)(2,1)S(1)} all-to-all(bf16[16,8,256]{2,0,1:T(8,128)(2,1)S(1)} %copy.34), channel_id=1, replica_groups=mesh['seq'=8,'chan'=4] {'seq'}, dimensions={1} | all-to-all | bytes 131072 | tf_op jit(solution)/shard_map/all_to_all | solution.py:138
  53.6 0.0 copy-done.2
  53.6 0.1 fusion.77
  53.7 13.9 %all_gather.7 = bf16[256,512]{0,1:T(8,128)(2,1)S(1)} all-gather(bf16[256,128]{0,1:T(8,128)(2,1)S(1)} %fusion.77), channel_id=1, replica_groups=mesh['seq'=8,'chan'=4] {'chan'}, dimensions={1}, use_global_device_ids=true | all-gather | bytes 327680 | tf_op jit(solution)/shard_map/all_gather | solution.py:22
  67.7 0.0 copy-done.1
  67.7 0.9 %convolution_convert_fusion.1 = bf16[256,128]{1,0:T(8,128)(2,1)} fusion(bf16[256,512]{0,1:T(8,128)(2,1)S(1)} %all_gather.7, bf16[512,128]{1,0:T(8,128)(2,1)S(1)} %copy-done.1), kind=kOutput, calls=%fused_computation.11 | convolution fusion | flops 33587200 | bytes 458752 | tf_op jit(solution)/shard_map/dot_general | solution.py:145
  (18 shorter events, 0.2 us)
Async XLA Ops:
  0.0 14.8 %copy-start = (bf16[3,512,128]{2,1,0:T(8,128)(2,1)S(1)}, bf16[3,512,128]{2,1,0:T(8,128)(2,1)}, u32[]{:S(2)}) copy-start(bf16[3,512,128]{2,1,0:T(8,128)(2,1)} %param.7) | copy-start | bytes 1179652
  15.8 8.7 %all-to-all-start = ((bf16[8,16,256]{2,1,0:T(8,128)(2,1)}), bf16[8,16,256]{2,1,0:T(8,128)(2,1)S(1)}, u32[]{:S(2)}, u32[]{:S(2)}) async-start(bf16[8,16,256]{2,1,0:T(8,128)(2,1)} %bitcast.6), calls=%async_computation | async-start | bytes 131072 | tf_op jit(solution)/shard_map/all_to_all | solution.py:127
  43.4 10.2 %copy-start.2 = (f32[128]{0:T(128)S(1)}, f32[128]{0:T(128)}, u32[]{:S(2)}) copy-start(f32[128]{0:T(128)} %param.11) | copy-start | bytes 1540
  43.4 24.2 %copy-start.1 = (bf16[512,128]{1,0:T(8,128)(2,1)S(1)}, bf16[512,128]{1,0:T(8,128)(2,1)}, u32[]{:S(2)}) copy-start(bf16[512,128]{1,0:T(8,128)(2,1)} %param.8) | copy-start | bytes 393220
where the time goes:
time: 68.9 us; the launch traced here: 68.6 us
  blocking collectives  36.1 us (52%)
  matrix products  16.2 us (24%)
  local copies, waits for them, and re-layouts  6.53 us (9%)
  starting transfers between devices  3.72 us (5%)
  waiting for transfers between devices  3.06 us (4%)
  other arithmetic  2.64 us (4%)
    all_gather x2, blocking collectives, fold_channels(): lax.all_gather(activations, 'chan', axis=1, tiled=True)  28.7 us
    all_to_all x1, blocking collectives, on_device(): lax.all_to_all(for_sending(flat_result), 'seq', split_axis=1, concat_axis...  7.4 us
    all_to_all x1, starting transfers between devices, on_device(): lax.all_to_all(product.T.astype(jnp.bfloat16), 'seq', split_axis=0, conca...  3.72 us
    dot_general x1, matrix products, middle_pass(): jnp.einsum('qb,kbc->kqc', dft_imag, real_part, precision=highest)  3.54 us
    all_to_all x1, waiting for transfers between devices, on_device(): lax.all_to_all(product.T.astype(jnp.bfloat16), 'seq', split_axis=0, conca...  3.06 us
    reshape x1, local copies, waits for them, and re-layouts, inverse_outer(): flat_imag = imag_part.reshape(outer, column_count * chan_count)  1.56 us
    reshape x1, local copies, waits for them, and re-layouts, inverse_outer(): flat_real = real_part.reshape(outer, column_count * chan_count)  1.56 us
    dot_general x1, matrix products, middle_pass(): jnp.einsum('qb,kqc->kbc', dft_real, prod_imag, precision=highest)  1.55 us
  transfers between devices with their start and end apart: 1, of which 1 were waited for; matrix products, arithmetic and copies ran while one was open for 3% of the time, Pallas kernels for 0%

commit v1 on v0

v1 whole, which is shorter than its diff:
```python
import functools

import jax
import jax.numpy as jnp
from jax import lax
from jax.experimental import pallas as pl
from jax.experimental.pallas import tpu as pltpu
from jax.sharding import PartitionSpec as P

MESH = pl.DeviceIdType.MESH
SUBLANES = 8
PIECES = 2
RIGHT, LEFT = 0, 1


def block_kernel(
    chan_count,
    seq_count,
    tok_ref,
    win_ref,
    wout_ref,
    rate_ref,
    res_ref,
    skip_ref,
    out_ref,
    tok_all,
    mix_all,
    win,
    wout,
    rate,
    res,
    skip,
    acc,
    acc_out,
    product,
    conv,
    local_state,
    entry_state,
    states,
    carry,
    decay_rows,
    weight_rows,
    local_sem,
    tok_send,
    tok_recv,
    mix_send,
    mix_recv,
    state_send,
    state_recv,
):
    place = lax.axis_index("chan")
    block = lax.axis_index("seq")
    positions, width = tok_ref.shape
    modes = rate_ref.shape[0]
    rows = positions // PIECES
    run = rows // SUBLANES
    run_count = positions // run

    barrier = pltpu.get_barrier_semaphore()
    has_left, has_right = place > 0, place < chan_count - 1

    def greet(axis, index):
        pl.semaphore_signal(barrier, inc=1, device_id={axis: index}, device_id_type=MESH)

    @pl.when(has_left)
    def _():
        greet("chan", place - 1)

    @pl.when(has_right)
    def _():
        greet("chan", place + 1)

    for distance in range(1, seq_count):

        @pl.when(block >= distance)
        def _():
            greet("seq", block - distance)

    own_tokens = pltpu.make_async_copy(tok_ref, tok_all.at[place], local_sem.at[0])
    own_tokens.start()
    win_copies = [
        pltpu.make_async_copy(
            win_ref.at[index], win.at[:, pl.ds(index * width, width)], local_sem.at[1 + index]
        )
        for index in range(3)
    ]
    for copy in win_copies:
        copy.start()
    small_copies = [
        pltpu.make_async_copy(rate_ref, rate, local_sem.at[4]),
        pltpu.make_async_copy(res_ref, res, local_sem.at[5]),
        pltpu.make_async_copy(skip_ref, skip, local_sem.at[6]),
    ]
    for copy in small_copies:
        copy.start()
    wout_copy = pltpu.make_async_copy(wout_ref, wout, local_sem.at[7])
    wout_copy.start()

    pl.semaphore_wait(
        barrier,
        seq_count - 1 - block + has_left.astype(jnp.int32) + has_right.astype(jnp.int32),
    )

    def span(piece):
        return pl.ds(piece * rows, rows)

    def hop(buffer, sends, recvs, way, step, piece, source=None):
        owner = place - step if way == RIGHT else place + step
        target = place + 1 if way == RIGHT else place - 1
        landing = buffer.at[owner, span(piece)]
        return pltpu.make_async_remote_copy(
            src_ref=landing if source is None else source.at[span(piece)],
            dst_ref=landing,
            send_sem=sends.at[way, step, piece],
            recv_sem=recvs.at[way, step, piece],
            device_id={"chan": target},
            device_id_type=MESH,
        )

    def sends_at(way, step):
        if way == RIGHT:
            return jnp.logical_and(place >= step, has_right)
        return jnp.logical_and(place + step < chan_count, has_left)

    def gets_at(way, step):
        return place > step if way == RIGHT else place + step + 1 < chan_count

    def send_own(buffer, sends, recvs, piece, source=None):
        for way in (RIGHT, LEFT):

            @pl.when(sends_at(way, 0))
            def _():
                hop(buffer, sends, recvs, way, 0, piece, source).start()

    def collect(buffer, sends, recvs, use):
        for step in range(chan_count - 1):
            for piece in range(PIECES):
                for way in (RIGHT, LEFT):

                    @pl.when(gets_at(way, step))
                    def _():
                        hop(buffer, sends, recvs, way, step, piece).wait_recv()

                    if step + 1 < chan_count - 1:

                        @pl.when(sends_at(way, step + 1))
                        def _():
                            hop(buffer, sends, recvs, way, step + 1, piece).start()

                for way in (RIGHT, LEFT):

                    @pl.when(gets_at(way, step))
                    def _():
                        use(place - step - 1 if way == RIGHT else place + step + 1, piece)

    def finish_sends(buffer, sends, recvs):
        for step in range(chan_count - 1):
            for piece in range(PIECES):
                for way in (RIGHT, LEFT):

                    @pl.when(sends_at(way, step))
                    def _():
                        hop(buffer, sends, recvs, way, step, piece).wait_send()

    for piece in range(PIECES):
        send_own(tok_all, tok_send, tok_recv, piece, tok_ref)

    for copy in small_copies:
        copy.wait()
    rates = rate[...]
    decay = jnp.exp(-rates)
    run_decay = jnp.exp(-rates * run)
    block_decay = jnp.exp(-rates * positions)
    weights = res[...] * jnp.sqrt(2.0 * rates)
    for mode in range(modes):
        decay_rows[mode] = jnp.broadcast_to(decay[mode : mode + 1], (SUBLANES, width))
        weight_rows[mode] = jnp.broadcast_to(weights[mode : mode + 1], (SUBLANES, width))

    def weight_span(owner):
        return pl.ds(pl.multiple_of(owner * width, width), width)

    own_tokens.wait()
    for copy in win_copies:
        copy.wait()
    acc[...] = jnp.dot(
        tok_all[place], win[weight_span(place)], preferred_element_type=jnp.float32
    )

    def project(owner, piece):
        acc[span(piece)] += jnp.dot(
            tok_all[owner, span(piece)],
            win[weight_span(owner)],
            preferred_element_type=jnp.float32,
        )

    collect(tok_all, tok_send, tok_recv, project)
    keys = acc[:, width : 2 * width].astype(jnp.bfloat16).astype(jnp.float32)
    values = acc[:, 2 * width :].astype(jnp.bfloat16).astype(jnp.float32)
    product[...] = keys * values

    def at_offset(piece, offset):
        return pl.ds(piece * rows + offset, SUBLANES, stride=run)

    decay_all = decay_rows[...]
    for piece in range(PIECES):
        state = jnp.zeros((modes, SUBLANES, width), jnp.float32)
        for offset in range(run):
            state = state * decay_all + product[at_offset(piece, offset)][None]
        for mode in range(modes):
            local_state[pl.ds(mode * run_count + piece * SUBLANES, SUBLANES)] = state[mode]

    def run_states(index):
        return pl.ds(index, modes, stride=run_count)

    total = local_state[run_states(0)]
    for index in range(1, run_count):
        total = total * run_decay + local_state[run_states(index)]
    states[block] = total

    def state_hop(distance):
        return pltpu.make_async_remote_copy(
            src_ref=states.at[block],
            dst_ref=states.at[block],
            send_sem=state_send.at[distance],
            recv_sem=state_recv.at[distance],
            device_id={"seq": block + distance},
            device_id_type=MESH,
        )

    for distance in range(1, seq_count):

        @pl.when(block + distance < seq_count)
        def _():
            state_hop(distance).start()

    carry[...] = jnp.zeros_like(carry)
    for distance in range(seq_count - 1, 0, -1):

        @pl.when(block >= distance)
        def _():
            pltpu.make_async_remote_copy(
                src_ref=states.at[block - distance],
                dst_ref=states.at[block - distance],
                send_sem=state_send.at[distance],
                recv_sem=state_recv.at[distance],
                device_id={"seq": block - distance},
                device_id_type=MESH,
            ).wait_recv()
            carry[...] = carry[...] * block_decay + states[block - distance]

    entering = carry[...]
    for index in range(run_count):
        entry_state[run_states(index)] = entering
        if index + 1 < run_count:
            entering = entering * run_decay + local_state[run_states(index)]

    weight_all = weight_rows[...]
    for piece in range(PIECES):
        state = jnp.stack(
            [
                entry_state[pl.ds(mode * run_count + piece * SUBLANES, SUBLANES)]
                for mode in range(modes)
            ]
        )
        for offset in range(run):
            state = state * decay_all + product[at_offset(piece, offset)][None]
            conv[at_offset(piece, offset)] = jnp.sum(state * weight_all, axis=0)
        query = acc[span(piece), :width].astype(jnp.bfloat16).astype(jnp.float32)
        mixed = query * (conv[span(piece)] + skip[...] * product[span(piece)])
        mix_all[place, span(piece)] = mixed.astype(jnp.bfloat16)
        send_own(mix_all, mix_send, mix_recv, piece)

    wout_copy.wait()
    acc_out[...] = jnp.dot(
        mix_all[place], wout[weight_span(place)], preferred_element_type=jnp.float32
    )

    def output(owner, piece):
        acc_out[span(piece)] += jnp.dot(
            mix_all[owner, span(piece)],
            wout[weight_span(owner)],
            preferred_element_type=jnp.float32,
        )

    collect(mix_all, mix_send, mix_recv, output)
    out_ref[...] = acc_out[...].astype(out_ref.dtype)

    finish_sends(tok_all, tok_send, tok_recv)
    finish_sends(mix_all, mix_send, mix_recv)
    for distance in range(1, seq_count):

        @pl.when(block + distance < seq_count)
        def _():
            state_hop(distance).wait_send()


def on_device(tokens, in_weight, out_weight, decay_rates, residues, skip_gain):
    chan_count, seq_count = lax.axis_size("chan"), lax.axis_size("seq")
    positions, width = tokens.shape
    modes = decay_rates.shape[0]
    channels = out_weight.shape[0]
    run_count = PIECES * SUBLANES
    hops = pltpu.SemaphoreType.DMA((2, max(chan_count - 1, 1), PIECES))
    return pl.pallas_call(
        functools.partial(block_kernel, chan_count, seq_count),
        out_shape=jax.ShapeDtypeStruct((positions, width), jnp.bfloat16),
        in_specs=[pl.BlockSpec(memory_space=pl.ANY)] * 6,
        out_specs=pl.BlockSpec(memory_space=pltpu.VMEM),
        scratch_shapes=[
            pltpu.VMEM((chan_count, positions, width), jnp.bfloat16),
            pltpu.VMEM((chan_count, positions, width), jnp.bfloat16),
            pltpu.VMEM((channels, 3 * width), jnp.bfloat16),
            pltpu.VMEM((channels, width), jnp.bfloat16),
            pltpu.VMEM((modes, width), jnp.float32),
            pltpu.VMEM((modes, width), jnp.float32),
            pltpu.VMEM((1, width), jnp.float32),
            pltpu.VMEM((positions, 3 * width), jnp.float32),
            pltpu.VMEM((positions, width), jnp.float32),
            pltpu.VMEM((positions, width), jnp.float32),
            pltpu.VMEM((positions, width), jnp.float32),
            pltpu.VMEM((modes * run_count, width), jnp.float32),
            pltpu.VMEM((modes * run_count, width), jnp.float32),
            pltpu.VMEM((seq_count, modes, width), jnp.float32),
            pltpu.VMEM((modes, width), jnp.float32),
            pltpu.VMEM((modes, SUBLANES, width), jnp.float32),
            pltpu.VMEM((modes, SUBLANES, width), jnp.float32),
            pltpu.SemaphoreType.DMA((8,)),
            hops,
            hops,
            hops,
            hops,
            pltpu.SemaphoreType.DMA((seq_count,)),
            pltpu.SemaphoreType.DMA((seq_count,)),
        ],
        compiler_params=pltpu.CompilerParams(
            collective_id=0, has_side_effects=True, vmem_limit_bytes=32 * 1024 * 1024
        ),
        name="hyena_block",
    )(tokens, in_weight, out_weight, decay_rates, residues, skip_gain.reshape(1, width))


def solution(mesh):
    return jax.shard_map(
        on_device,
        mesh=mesh,
        in_specs=(
            P("seq", "chan"),
            P(None, None, "chan"),
            P(None, "chan"),
            P(None, "chan"),
            P(None, "chan"),
            P("chan"),
        ),
        out_specs=P("seq", "chan"),
        check_vma=False,
    )
```

time: 68.9 us -> 31.6 us (0.46)
  the two profiles are of different devices: /device:TPU:0 before, /device:TPU:4 now
where the time goes in v1:
time: 31.6 us; the launch traced here: 31.3 us
  Pallas kernels  25.8 us (82%)
  local copies, waits for them, and re-layouts  5.42 us (17%)
    pallas_call x1, Pallas kernels, on_device(): pl.pallas_call(functools.partial(block_kernel, chan_count, seq_count), ou...  25.8 us
    unnamed x13, local copies, waits for them, and re-layouts  5.42 us

profile of v1, /device:TPU:4, one launch (start us, length us, event | category | flops | bytes accessed | tf_op | source)
XLA Modules:
  0.0 31.3 jit_solution(5326367823367008174)
XLA Ops:
  0.0 0.0 copy-start.5
  0.0 0.7 %copy-done.5 = f32[128]{0:T(128)S(1)} copy-done((f32[128]{0:T(128)S(1)}, f32[128]{0:T(128)}, u32[]{:S(2)}) %copy-start.5) | copy-done | bytes 536
  0.7 0.0 copy-start
  0.7 1.0 %copy-done = bf16[3,512,128]{2,1,0:T(8,128)(2,1)S(1)} copy-done((bf16[3,512,128]{2,1,0:T(8,128)(2,1)S(1)}, bf16[3,512,128]{2,1,0:T(8,128)(2,1)}, u32[]{:S(2)}) %copy-start) | copy-done | bytes 393240
  1.7 0.0 copy-start.1
  1.7 0.9 %copy-done.1 = bf16[512,128]{1,0:T(8,128)(2,1)S(1)} copy-done((bf16[512,128]{1,0:T(8,128)(2,1)S(1)}, bf16[512,128]{1,0:T(8,128)(2,1)}, u32[]{:S(2)}) %copy-start.1) | copy-done | bytes 131096
  2.6 0.0 copy-start.2
  2.6 0.8 %copy-done.2 = bf16[256,128]{1,0:T(8,128)(2,1)S(1)} copy-done((bf16[256,128]{1,0:T(8,128)(2,1)S(1)}, bf16[256,128]{1,0:T(8,128)(2,1)}, u32[]{:S(2)}) %copy-start.2) | copy-done | bytes 65560
  3.4 0.0 copy-start.3
  3.4 0.7 %copy-done.3 = f32[16,128]{1,0:T(8,128)S(1)} copy-done((f32[16,128]{1,0:T(8,128)S(1)}, f32[16,128]{1,0:T(8,128)}, u32[]{:S(2)}) %copy-start.3) | copy-done | bytes 8216
  4.1 0.0 copy-start.4
  4.1 0.7 %copy-done.4 = f32[16,128]{1,0:T(8,128)S(1)} copy-done((f32[16,128]{1,0:T(8,128)S(1)}, f32[16,128]{1,0:T(8,128)}, u32[]{:S(2)}) %copy-start.4) | copy-done | bytes 8216
  4.8 25.8 %hyena_block.1 = bf16[256,128]{1,0:T(8,128)(2,1)S(1)} custom-call(bf16[256,128]{1,0:T(8,128)(2,1)S(1)} %copy-done.2, bf16[3,512,128]{2,1,0:T(8,128)(2,1)S(1)} %copy-done, bf16[512,128]{1,0:T(8,128)(2,1)S(1)} %copy-done.1, f32[16,128]{1,0:T(8,128)S(1)} %copy-done.3, f32[16,128]{1,0:T(8,128)S(1)} %copy-done.4, f32[1,128]{1,0:T(1,128)S(1)} %bitcast.1), custom_call_target="tpu_custom_call" | custom-call | tf_op jit(solution)/shard_map/hyena_block/pallas_call | solution.py:304
  30.6 0.6 %copy.8 = bf16[256,128]{1,0:T(8,128)(2,1)} copy(bf16[256,128]{1,0:T(8,128)(2,1)S(1)} %hyena_block.1) | data formatting | bytes 131072
Async XLA Ops:
  0.0 0.7 %copy-start.5 = (f32[128]{0:T(128)S(1)}, f32[128]{0:T(128)}, u32[]{:S(2)}) copy-start(f32[128]{0:T(128)} %param.11) | copy-start | bytes 1540
  0.7 1.0 %copy-start = (bf16[3,512,128]{2,1,0:T(8,128)(2,1)S(1)}, bf16[3,512,128]{2,1,0:T(8,128)(2,1)}, u32[]{:S(2)}) copy-start(bf16[3,512,128]{2,1,0:T(8,128)(2,1)} %win_ref.1) | copy-start | bytes 1179652
  1.7 0.9 %copy-start.1 = (bf16[512,128]{1,0:T(8,128)(2,1)S(1)}, bf16[512,128]{1,0:T(8,128)(2,1)}, u32[]{:S(2)}) copy-start(bf16[512,128]{1,0:T(8,128)(2,1)} %wout_ref.1) | copy-start | bytes 393220
  2.6 0.8 %copy-start.2 = (bf16[256,128]{1,0:T(8,128)(2,1)S(1)}, bf16[256,128]{1,0:T(8,128)(2,1)}, u32[]{:S(2)}) copy-start(bf16[256,128]{1,0:T(8,128)(2,1)} %tok_ref.1) | copy-start | bytes 196612
  3.4 0.7 %copy-start.3 = (f32[16,128]{1,0:T(8,128)S(1)}, f32[16,128]{1,0:T(8,128)}, u32[]{:S(2)}) copy-start(f32[16,128]{1,0:T(8,128)} %rate_ref.1) | copy-start | bytes 24580
  4.1 0.7 %copy-start.4 = (f32[16,128]{1,0:T(8,128)S(1)}, f32[16,128]{1,0:T(8,128)}, u32[]{:S(2)}) copy-start(f32[16,128]{1,0:T(8,128)} %res_ref.1) | copy-start | bytes 24580

commit v2 on v1

--- a/solution.py
+++ b/solution.py
@@ -10,7 +10,6 @@
 MESH = pl.DeviceIdType.MESH
 SUBLANES = 8
 PIECES = 2
-RIGHT, LEFT = 0, 1
 
 
 def block_kernel(
@@ -30,8 +29,7 @@
     rate,
     res,
     skip,
-    acc,
-    acc_out,
+    query,
     product,
     conv,
     local_state,
@@ -57,18 +55,12 @@
     run_count = positions // run
 
     barrier = pltpu.get_barrier_semaphore()
-    has_left, has_right = place > 0, place < chan_count - 1
 
     def greet(axis, index):
         pl.semaphore_signal(barrier, inc=1, device_id={axis: index}, device_id_type=MESH)
 
-    @pl.when(has_left)
-    def _():
-        greet("chan", place - 1)
-
-    @pl.when(has_right)
-    def _():
-        greet("chan", place + 1)
+    for distance in range(1, chan_count):
+        greet("chan", lax.rem(place + distance, chan_count))
 
     for distance in range(1, seq_count):
 
@@ -96,71 +88,43 @@
     wout_copy = pltpu.make_async_copy(wout_ref, wout, local_sem.at[7])
     wout_copy.start()
 
-    pl.semaphore_wait(
-        barrier,
-        seq_count - 1 - block + has_left.astype(jnp.int32) + has_right.astype(jnp.int32),
-    )
+    pl.semaphore_wait(barrier, seq_count - 1 - block + chan_count - 1)
 
     def span(piece):
         return pl.ds(piece * rows, rows)
 
-    def hop(buffer, sends, recvs, way, step, piece, source=None):
-        owner = place - step if way == RIGHT else place + step
-        target = place + 1 if way == RIGHT else place - 1
-        landing = buffer.at[owner, span(piece)]
+    def hop(buffer, sends, recvs, distance, piece, source=None):
+        landing = buffer.at[place, span(piece)]
         return pltpu.make_async_remote_copy(
             src_ref=landing if source is None else source.at[span(piece)],
             dst_ref=landing,
-            send_sem=sends.at[way, step, piece],
-            recv_sem=recvs.at[way, step, piece],
-            device_id={"chan": target},
+            send_sem=sends.at[distance, piece],
+            recv_sem=recvs.at[distance, piece],
+            device_id={"chan": lax.rem(place + distance, chan_count)},
             device_id_type=MESH,
         )
 
-    def sends_at(way, step):
-        if way == RIGHT:
-            return jnp.logical_and(place >= step, has_right)
-        return jnp.logical_and(place + step < chan_count, has_left)
-
-    def gets_at(way, step):
-        return place > step if way == RIGHT else place + step + 1 < chan_count
-
     def send_own(buffer, sends, recvs, piece, source=None):
-        for way in (RIGHT, LEFT):
-
-            @pl.when(sends_at(way, 0))
-            def _():
-                hop(buffer, sends, recvs, way, 0, piece, source).start()
-
-    def collect(buffer, sends, recvs, use):
-        for step in range(chan_count - 1):
-            for piece in range(PIECES):
-                for way in (RIGHT, LEFT):
-
-                    @pl.when(gets_at(way, step))
-                    def _():
-                        hop(buffer, sends, recvs, way, step, piece).wait_recv()
-
-                    if step + 1 < chan_count - 1:
-
-                        @pl.when(sends_at(way, step + 1))
-                        def _():
-                            hop(buffer, sends, recvs, way, step + 1, piece).start()
-
-                for way in (RIGHT, LEFT):
-
-                    @pl.when(gets_at(way, step))
-                    def _():
-                        use(place - step - 1 if way == RIGHT else place + step + 1, piece)
-
-    def finish_sends(buffer, sends, recvs):
-        for step in range(chan_count - 1):
-            for piece in range(PIECES):
-                for way in (RIGHT, LEFT):
-
-                    @pl.when(sends_at(way, step))
-                    def _():
-                        hop(buffer, sends, recvs, way, step, piece).wait_send()
+        for distance in range(1, chan_count):
+            hop(buffer, sends, recvs, distance, piece, source).start()
+
+    def collect(buffer, sends, recvs, piece):
+        for distance in range(1, chan_count):
+            landing = buffer.at[lax.rem(place + chan_count - distance, chan_count), span(piece)]
+            pltpu.make_async_remote_copy(
+                src_ref=landing,
+                dst_ref=landing,
+                send_sem=sends.at[distance, piece],
+                recv_sem=recvs.at[distance, piece],
+                device_id={"chan": lax.rem(place + distance, chan_count)},
+                device_id_type=MESH,
+            ).wait_recv()
+        return jnp.concatenate([buffer[owner, span(piece)] for owner in range(chan_count)], axis=1)
+
+    def finish_sends(buffer, sends, recvs, source=None):
+        for piece in range(PIECES):
+            for distance in range(1, chan_count):
+                hop(buffer, sends, recvs, distance, piece, source).wait_send()
 
     for piece in range(PIECES):
         send_own(tok_all, tok_send, tok_recv, piece, tok_ref)
@@ -175,34 +139,23 @@
     for mode in range(modes):
         decay_rows[mode] = jnp.broadcast_to(decay[mode : mode + 1], (SUBLANES, width))
         weight_rows[mode] = jnp.broadcast_to(weights[mode : mode + 1], (SUBLANES, width))
-
-    def weight_span(owner):
-        return pl.ds(pl.multiple_of(owner * width, width), width)
+    decay_all = decay_rows[...]
 
     own_tokens.wait()
     for copy in win_copies:
         copy.wait()
-    acc[...] = jnp.dot(
-        tok_all[place], win[weight_span(place)], preferred_element_type=jnp.float32
-    )
-
-    def project(owner, piece):
-        acc[span(piece)] += jnp.dot(
-            tok_all[owner, span(piece)],
-            win[weight_span(owner)],
-            preferred_element_type=jnp.float32,
-        )
-
-    collect(tok_all, tok_send, tok_recv, project)
-    keys = acc[:, width : 2 * width].astype(jnp.bfloat16).astype(jnp.float32)
-    values = acc[:, 2 * width :].astype(jnp.bfloat16).astype(jnp.float32)
-    product[...] = keys * values
 
     def at_offset(piece, offset):
         return pl.ds(piece * rows + offset, SUBLANES, stride=run)
 
-    decay_all = decay_rows[...]
     for piece in range(PIECES):
+        projected = jnp.dot(
+            collect(tok_all, tok_send, tok_recv, piece),
+            win[...],
+            preferred_element_type=jnp.float32,
+        ).astype(jnp.bfloat16).astype(jnp.float32)
+        query[span(piece)] = projected[:, :width]
+        product[span(piece)] = projected[:, width : 2 * width] * projected[:, 2 * width :]
         state = jnp.zeros((modes, SUBLANES, width), jnp.float32)
         for offset in range(run):
             state = state * decay_all + product[at_offset(piece, offset)][None]
@@ -265,27 +218,19 @@
         for offset in range(run):
             state = state * decay_all + product[at_offset(piece, offset)][None]
             conv[at_offset(piece, offset)] = jnp.sum(state * weight_all, axis=0)
-        query = acc[span(piece), :width].astype(jnp.bfloat16).astype(jnp.float32)
-        mixed = query * (conv[span(piece)] + skip[...] * product[span(piece)])
+        mixed = query[span(piece)] * (conv[span(piece)] + skip[...] * product[span(piece)])
         mix_all[place, span(piece)] = mixed.astype(jnp.bfloat16)
         send_own(mix_all, mix_send, mix_recv, piece)
 
     wout_copy.wait()
-    acc_out[...] = jnp.dot(
-        mix_all[place], wout[weight_span(place)], preferred_element_type=jnp.float32
-    )
-
-    def output(owner, piece):
-        acc_out[span(piece)] += jnp.dot(
-            mix_all[owner, span(piece)],
-            wout[weight_span(owner)],
+    for piece in range(PIECES):
+        out_ref[span(piece)] = jnp.dot(
+            collect(mix_all, mix_send, mix_recv, piece),
+            wout[...],
             preferred_element_type=jnp.float32,
-        )
-
-    collect(mix_all, mix_send, mix_recv, output)
-    out_ref[...] = acc_out[...].astype(out_ref.dtype)
-
-    finish_sends(tok_all, tok_send, tok_recv)
+        ).astype(out_ref.dtype)
+
+    finish_sends(tok_all, tok_send, tok_recv, tok_ref)
     finish_sends(mix_all, mix_send, mix_recv)
     for distance in range(1, seq_count):
 
@@ -300,11 +245,11 @@
     modes = decay_rates.shape[0]
     channels = out_weight.shape[0]
     run_count = PIECES * SUBLANES
-    hops = pltpu.SemaphoreType.DMA((2, max(chan_count - 1, 1), PIECES))
+    hops = pltpu.SemaphoreType.DMA((chan_count, PIECES))
     return pl.pallas_call(
         functools.partial(block_kernel, chan_count, seq_count),
         out_shape=jax.ShapeDtypeStruct((positions, width), jnp.bfloat16),
-        in_specs=[pl.BlockSpec(memory_space=pl.ANY)] * 6,
+        in_specs=[pl.BlockSpec(memory_space=pltpu.HBM)] * 6,
         out_specs=pl.BlockSpec(memory_space=pltpu.VMEM),
         scratch_shapes=[
             pltpu.VMEM((chan_count, positions, width), jnp.bfloat16),
@@ -314,7 +259,6 @@
             pltpu.VMEM((modes, width), jnp.float32),
             pltpu.VMEM((modes, width), jnp.float32),
             pltpu.VMEM((1, width), jnp.float32),
-            pltpu.VMEM((positions, 3 * width), jnp.float32),
             pltpu.VMEM((positions, width), jnp.float32),
             pltpu.VMEM((positions, width), jnp.float32),
             pltpu.VMEM((positions, width), jnp.float32),
@@ -333,7 +277,7 @@
             pltpu.SemaphoreType.DMA((seq_count,)),
         ],
         compiler_params=pltpu.CompilerParams(
-            collective_id=0, has_side_effects=True, vmem_limit_bytes=32 * 1024 * 1024
+            collective_id=0, has_side_effects=True, vmem_limit_bytes=56 * 1024 * 1024
         ),
         name="hyena_block",
     )(tokens, in_weight, out_weight, decay_rates, residues, skip_gain.reshape(1, width))

time: 31.6 us -> 24.4 us (0.77)
  local copies, waits for them, and re-layouts: 5.42 us -> 1.47 us
  Pallas kernels: 25.8 us -> 22.7 us
    unnamed x13 -> x1, local copies, waits for them, and re-layouts: 5.42 us -> 1.47 us
    pallas_call x1, Pallas kernels: 25.8 us -> 22.7 us  [on_device(): pl.pallas_call(functools.partial(block_kernel, chan_count, seq_count), ou...]
where the time goes in v2:
time: 24.4 us; the launch traced here: 24.2 us
  Pallas kernels  22.7 us (93%)
  local copies, waits for them, and re-layouts  1.47 us (6%)
    pallas_call x1, Pallas kernels, on_device(): pl.pallas_call(functools.partial(block_kernel, chan_count, seq_count), ou...  22.7 us
    unnamed x1, local copies, waits for them, and re-layouts  1.47 us

profile of v2, /device:TPU:4, one launch (start us, length us, event | category | flops | bytes accessed | tf_op | source)
XLA Modules:
  0.0 24.2 jit_solution(17050779313659936749)
XLA Ops:
  0.0 22.7 %hyena_block.1 = bf16[256,128]{1,0:T(8,128)(2,1)} custom-call(bf16[256,128]{1,0:T(8,128)(2,1)} %tok_ref.1, bf16[3,512,128]{2,1,0:T(8,128)(2,1)} %win_ref.1, bf16[512,128]{1,0:T(8,128)(2,1)} %wout_ref.1, f32[16,128]{1,0:T(8,128)} %rate_ref.1, f32[16,128]{1,0:T(8,128)} %res_ref.1, f32[1,128]{1,0:T(1,128)} %bitcast.1), custom_call_target="tpu_custom_call" | custom-call | tf_op jit(solution)/shard_map/hyena_block/pallas_call | solution.py:249
  22.7 1.5 %copy.8 = bf16[256,128]{1,0:T(8,128)(2,1)} copy(bf16[256,128]{1,0:T(8,128)(2,1)} %hyena_block.1) | data formatting | bytes 131072

commit v3 on v2

--- a/solution.py
+++ b/solution.py
@@ -104,30 +104,84 @@
             device_id_type=MESH,
         )
 
-    def send_own(buffer, sends, recvs, piece, source=None):
-        for distance in range(1, chan_count):
-            hop(buffer, sends, recvs, distance, piece, source).start()
+    relays = []
+    if chan_count > 2:
+        relays = [(1, chan_count - 2, chan_count - 1), (chan_count - 1, 1, 0)]
+
+    def goes_direct(distance):
+        target = lax.rem(place + distance, chan_count)
+        direct = None
+        for step, relay, end in relays:
+            if distance == 2 * step % chan_count:
+                owner = (end - 2 * step) % chan_count
+                here = jnp.logical_not(jnp.logical_and(place == owner, target == end))
+                direct = here if direct is None else jnp.logical_and(direct, here)
+        return direct
+
+    def when(condition, action):
+        if condition is None:
+            action()
+        else:
+            pl.when(condition)(action)
+
+    near = sorted({1, chan_count - 1} - {0})
+    far = [distance for distance in range(2, chan_count - 1)]
+
+    def send_own(buffer, sends, recvs, piece, distances, source=None):
+        for distance in distances:
+            copy = hop(buffer, sends, recvs, distance, piece, source)
+            when(goes_direct(distance), copy.start)
+
+    def relay_hop(buffer, sends, recvs, piece, step, end):
+        landing = buffer.at[(end - 2 * step) % chan_count, span(piece)]
+        return pltpu.make_async_remote_copy(
+            src_ref=landing,
+            dst_ref=landing,
+            send_sem=sends.at[0, piece] if step == 1 else sends.at[chan_count, piece],
+            recv_sem=recvs.at[2 * step % chan_count, piece],
+            device_id={"chan": end},
+            device_id_type=MESH,
+        )
+
+    def arrival(buffer, sends, recvs, piece, distance):
+        landing = buffer.at[lax.rem(place + chan_count - distance, chan_count), span(piece)]
+        return pltpu.make_async_remote_copy(
+            src_ref=landing,
+            dst_ref=landing,
+            send_sem=sends.at[distance, piece],
+            recv_sem=recvs.at[distance, piece],
+            device_id={"chan": lax.rem(place + distance, chan_count)},
+            device_id_type=MESH,
+        )
+
+    def pass_on(buffer, sends, recvs):
+        for piece in range(PIECES):
+            for step, relay, end in relays:
+
+                @pl.when(place == relay)
+                def _():
+                    arrival(buffer, sends, recvs, piece, step).wait_recv()
+                    relay_hop(buffer, sends, recvs, piece, step, end).start()
 
     def collect(buffer, sends, recvs, piece):
-        for distance in range(1, chan_count):
-            landing = buffer.at[lax.rem(place + chan_count - distance, chan_count), span(piece)]
-            pltpu.make_async_remote_copy(
-                src_ref=landing,
-                dst_ref=landing,
-                send_sem=sends.at[distance, piece],
-                recv_sem=recvs.at[distance, piece],
-                device_id={"chan": lax.rem(place + distance, chan_count)},
-                device_id_type=MESH,
-            ).wait_recv()
+        passed_on = {step: relay for step, relay, _ in relays}
+        for distance in near + far:
+            others = place != passed_on[distance] if distance in passed_on else None
+            when(others, arrival(buffer, sends, recvs, piece, distance).wait_recv)
         return jnp.concatenate([buffer[owner, span(piece)] for owner in range(chan_count)], axis=1)
 
     def finish_sends(buffer, sends, recvs, source=None):
         for piece in range(PIECES):
-            for distance in range(1, chan_count):
-                hop(buffer, sends, recvs, distance, piece, source).wait_send()
-
-    for piece in range(PIECES):
-        send_own(tok_all, tok_send, tok_recv, piece, tok_ref)
+            for distance in near + far:
+                copy = hop(buffer, sends, recvs, distance, piece, source)
+                when(goes_direct(distance), copy.wait_send)
+            for step, relay, end in relays:
+                copy = relay_hop(buffer, sends, recvs, piece, step, end)
+                pl.when(place == relay)(copy.wait_send)
+
+    for distances in (near, far):
+        for piece in range(PIECES):
+            send_own(tok_all, tok_send, tok_recv, piece, distances, tok_ref)
 
     for copy in small_copies:
         copy.wait()
@@ -144,6 +198,8 @@
     own_tokens.wait()
     for copy in win_copies:
         copy.wait()
+
+    pass_on(tok_all, tok_send, tok_recv)
 
     def at_offset(piece, offset):
         return pl.ds(piece * rows + offset, SUBLANES, stride=run)
@@ -220,9 +276,10 @@
             conv[at_offset(piece, offset)] = jnp.sum(state * weight_all, axis=0)
         mixed = query[span(piece)] * (conv[span(piece)] + skip[...] * product[span(piece)])
         mix_all[place, span(piece)] = mixed.astype(jnp.bfloat16)
-        send_own(mix_all, mix_send, mix_recv, piece)
+        send_own(mix_all, mix_send, mix_recv, piece, near + far)
 
     wout_copy.wait()
+    pass_on(mix_all, mix_send, mix_recv)
     for piece in range(PIECES):
         out_ref[span(piece)] = jnp.dot(
             collect(mix_all, mix_send, mix_recv, piece),
@@ -245,10 +302,18 @@
     modes = decay_rates.shape[0]
     channels = out_weight.shape[0]
     run_count = PIECES * SUBLANES
-    hops = pltpu.SemaphoreType.DMA((chan_count, PIECES))
+    operands = (
+        tokens,
+        in_weight,
+        out_weight,
+        decay_rates,
+        residues,
+        skip_gain.reshape(1, width),
+    )
+    hops = pltpu.SemaphoreType.DMA((chan_count + 1, PIECES))
     return pl.pallas_call(
         functools.partial(block_kernel, chan_count, seq_count),
-        out_shape=jax.ShapeDtypeStruct((positions, width), jnp.bfloat16),
+        out_shape=pltpu.VMEM((positions, width), jnp.bfloat16),
         in_specs=[pl.BlockSpec(memory_space=pltpu.HBM)] * 6,
         out_specs=pl.BlockSpec(memory_space=pltpu.VMEM),
         scratch_shapes=[
@@ -277,10 +342,10 @@
             pltpu.SemaphoreType.DMA((seq_count,)),
         ],
         compiler_params=pltpu.CompilerParams(
-            collective_id=0, has_side_effects=True, vmem_limit_bytes=56 * 1024 * 1024
+            collective_id=0, has_side_effects=True, vmem_limit_bytes=32 * 1024 * 1024
         ),
         name="hyena_block",
-    )(tokens, in_weight, out_weight, decay_rates, residues, skip_gain.reshape(1, width))
+    )(*(pltpu.with_memory_space_constraint(operand, pltpu.HBM) for operand in operands))
 
 
 def solution(mesh):

time: 24.4 us -> 22.5 us (0.922)
  Pallas kernels: 22.7 us -> 21.7 us
  local copies, waits for them, and re-layouts: 1.47 us -> 0.63 us
    pallas_call x1, Pallas kernels: 22.7 us -> 21.7 us  [on_device(): pl.pallas_call(functools.partial(block_kernel, chan_count, seq_count), ou...]
    unnamed x1, local copies, waits for them, and re-layouts: 1.47 us -> 0.63 us
where the time goes in v3:
time: 22.5 us; the launch traced here: 22.4 us
  Pallas kernels  21.7 us (96%)
  local copies, waits for them, and re-layouts  0.63 us (3%)
    pallas_call x1, Pallas kernels, on_device(): pl.pallas_call(functools.partial(block_kernel, chan_count, seq_count), ou...  21.7 us
    unnamed x1, local copies, waits for them, and re-layouts  0.63 us

profile of v3, /device:TPU:4, one launch (start us, length us, event | category | flops | bytes accessed | tf_op | source)
XLA Modules:
  0.0 22.4 jit_solution(1935586725306282238)
XLA Ops:
  0.0 21.7 %hyena_block.1 = bf16[256,128]{1,0:T(8,128)(2,1)S(1)} custom-call(bf16[256,128]{1,0:T(8,128)(2,1)} %tok_ref.1, bf16[3,512,128]{2,1,0:T(8,128)(2,1)} %win_ref.1, bf16[512,128]{1,0:T(8,128)(2,1)} %wout_ref.1, f32[16,128]{1,0:T(8,128)} %rate_ref.1, f32[16,128]{1,0:T(8,128)} %res_ref.1, f32[1,128]{1,0:T(1,128)} %bitcast.1), custom_call_target="tpu_custom_call" | custom-call | tf_op jit(solution)/shard_map/hyena_block/pallas_call | solution.py:314
  21.8 0.6 %copy.8 = bf16[256,128]{1,0:T(8,128)(2,1)} copy(bf16[256,128]{1,0:T(8,128)(2,1)S(1)} %hyena_block.1) | data formatting | bytes 131072

commit v4 on v3

--- a/solution.py
+++ b/solution.py
@@ -38,6 +38,7 @@
     carry,
     decay_rows,
     weight_rows,
+    carry_rows,
     local_sem,
     tok_send,
     tok_recv,
@@ -68,6 +69,100 @@
         def _():
             greet("seq", block - distance)
 
+    pl.semaphore_wait(barrier, seq_count - 1 - block + chan_count - 1)
+
+    def span(piece):
+        return pl.ds(piece * rows, rows)
+
+    def hop(buffer, sends, recvs, distance, piece, source=None):
+        landing = buffer.at[place, span(piece)]
+        return pltpu.make_async_remote_copy(
+            src_ref=landing if source is None else source.at[span(piece)],
+            dst_ref=landing,
+            send_sem=sends.at[distance, piece],
+            recv_sem=recvs.at[distance, piece],
+            device_id={"chan": lax.rem(place + distance, chan_count)},
+            device_id_type=MESH,
+        )
+
+    relays = []
+    if chan_count > 2:
+        relays = [(1, chan_count - 2, chan_count - 1), (chan_count - 1, 1, 0)]
+
+    def goes_direct(distance):
+        target = lax.rem(place + distance, chan_count)
+        direct = None
+        for step, relay, end in relays:
+            if distance == 2 * step % chan_count:
+                owner = (end - 2 * step) % chan_count
+                here = jnp.logical_not(jnp.logical_and(place == owner, target == end))
+                direct = here if direct is None else jnp.logical_and(direct, here)
+        return direct
+
+    def when(condition, action):
+        if condition is None:
+            action()
+        else:
+            pl.when(condition)(action)
+
+    near = sorted({1, chan_count - 1} - {0})
+    far = [distance for distance in range(2, chan_count - 1)]
+
+    def send_own(buffer, sends, recvs, piece, distances, source=None):
+        for distance in distances:
+            copy = hop(buffer, sends, recvs, distance, piece, source)
+            when(goes_direct(distance), copy.start)
+
+    def relay_hop(buffer, sends, recvs, piece, step, end):
+        landing = buffer.at[(end - 2 * step) % chan_count, span(piece)]
+        return pltpu.make_async_remote_copy(
+            src_ref=landing,
+            dst_ref=landing,
+            send_sem=sends.at[0, piece] if step == 1 else sends.at[chan_count, piece],
+            recv_sem=recvs.at[2 * step % chan_count, piece],
+            device_id={"chan": end},
+            device_id_type=MESH,
+        )
+
+    def arrival(buffer, sends, recvs, piece, distance):
+        landing = buffer.at[lax.rem(place + chan_count - distance, chan_count), span(piece)]
+        return pltpu.make_async_remote_copy(
+            src_ref=landing,
+            dst_ref=landing,
+            send_sem=sends.at[distance, piece],
+            recv_sem=recvs.at[distance, piece],
+            device_id={"chan": lax.rem(place + distance, chan_count)},
+            device_id_type=MESH,
+        )
+
+    def pass_on(buffer, sends, recvs):
+        for piece in range(PIECES):
+            for step, relay, end in relays:
+
+                @pl.when(place == relay)
+                def _():
+                    arrival(buffer, sends, recvs, piece, step).wait_recv()
+                    relay_hop(buffer, sends, recvs, piece, step, end).start()
+
+    def collect(buffer, sends, recvs, piece):
+        passed_on = {step: relay for step, relay, _ in relays}
+        for distance in near + far:
+            others = place != passed_on[distance] if distance in passed_on else None
+            when(others, arrival(buffer, sends, recvs, piece, distance).wait_recv)
+        return jnp.concatenate([buffer[owner, span(piece)] for owner in range(chan_count)], axis=1)
+
+    def finish_sends(buffer, sends, recvs, piece, source=None):
+        for distance in near + far:
+            copy = hop(buffer, sends, recvs, distance, piece, source)
+            when(goes_direct(distance), copy.wait_send)
+        for step, relay, end in relays:
+            copy = relay_hop(buffer, sends, recvs, piece, step, end)
+            pl.when(place == relay)(copy.wait_send)
+
+    for distances in (near, far):
+        for piece in range(PIECES):
+            send_own(tok_all, tok_send, tok_recv, piece, distances, tok_ref)
+
     own_tokens = pltpu.make_async_copy(tok_ref, tok_all.at[place], local_sem.at[0])
     own_tokens.start()
     win_copies = [
@@ -88,101 +183,6 @@
     wout_copy = pltpu.make_async_copy(wout_ref, wout, local_sem.at[7])
     wout_copy.start()
 
-    pl.semaphore_wait(barrier, seq_count - 1 - block + chan_count - 1)
-
-    def span(piece):
-        return pl.ds(piece * rows, rows)
-
-    def hop(buffer, sends, recvs, distance, piece, source=None):
-        landing = buffer.at[place, span(piece)]
-        return pltpu.make_async_remote_copy(
-            src_ref=landing if source is None else source.at[span(piece)],
-            dst_ref=landing,
-            send_sem=sends.at[distance, piece],
-            recv_sem=recvs.at[distance, piece],
-            device_id={"chan": lax.rem(place + distance, chan_count)},
-            device_id_type=MESH,
-        )
-
-    relays = []
-    if chan_count > 2:
-        relays = [(1, chan_count - 2, chan_count - 1), (chan_count - 1, 1, 0)]
-
-    def goes_direct(distance):
-        target = lax.rem(place + distance, chan_count)
-        direct = None
-        for step, relay, end in relays:
-            if distance == 2 * step % chan_count:
-                owner = (end - 2 * step) % chan_count
-                here = jnp.logical_not(jnp.logical_and(place == owner, target == end))
-                direct = here if direct is None else jnp.logical_and(direct, here)
-        return direct
-
-    def when(condition, action):
-        if condition is None:
-            action()
-        else:
-            pl.when(condition)(action)
-
-    near = sorted({1, chan_count - 1} - {0})
-    far = [distance for distance in range(2, chan_count - 1)]
-
-    def send_own(buffer, sends, recvs, piece, distances, source=None):
-        for distance in distances:
-            copy = hop(buffer, sends, recvs, distance, piece, source)
-            when(goes_direct(distance), copy.start)
-
-    def relay_hop(buffer, sends, recvs, piece, step, end):
-        landing = buffer.at[(end - 2 * step) % chan_count, span(piece)]
-        return pltpu.make_async_remote_copy(
-            src_ref=landing,
-            dst_ref=landing,
-            send_sem=sends.at[0, piece] if step == 1 else sends.at[chan_count, piece],
-            recv_sem=recvs.at[2 * step % chan_count, piece],
-            device_id={"chan": end},
-            device_id_type=MESH,
-        )
-
-    def arrival(buffer, sends, recvs, piece, distance):
-        landing = buffer.at[lax.rem(place + chan_count - distance, chan_count), span(piece)]
-        return pltpu.make_async_remote_copy(
-            src_ref=landing,
-            dst_ref=landing,
-            send_sem=sends.at[distance, piece],
-            recv_sem=recvs.at[distance, piece],
-            device_id={"chan": lax.rem(place + distance, chan_count)},
-            device_id_type=MESH,
-        )
-
-    def pass_on(buffer, sends, recvs):
-        for piece in range(PIECES):
-            for step, relay, end in relays:
-
-                @pl.when(place == relay)
-                def _():
-                    arrival(buffer, sends, recvs, piece, step).wait_recv()
-                    relay_hop(buffer, sends, recvs, piece, step, end).start()
-
-    def collect(buffer, sends, recvs, piece):
-        passed_on = {step: relay for step, relay, _ in relays}
-        for distance in near + far:
-            others = place != passed_on[distance] if distance in passed_on else None
-            when(others, arrival(buffer, sends, recvs, piece, distance).wait_recv)
-        return jnp.concatenate([buffer[owner, span(piece)] for owner in range(chan_count)], axis=1)
-
-    def finish_sends(buffer, sends, recvs, source=None):
-        for piece in range(PIECES):
-            for distance in near + far:
-                copy = hop(buffer, sends, recvs, distance, piece, source)
-                when(goes_direct(distance), copy.wait_send)
-            for step, relay, end in relays:
-                copy = relay_hop(buffer, sends, recvs, piece, step, end)
-                pl.when(place == relay)(copy.wait_send)
-
-    for distances in (near, far):
-        for piece in range(PIECES):
-            send_own(tok_all, tok_send, tok_recv, piece, distances, tok_ref)
-
     for copy in small_copies:
         copy.wait()
     rates = rate[...]
@@ -200,6 +200,9 @@
         copy.wait()
 
     pass_on(tok_all, tok_send, tok_recv)
+    elapsed = (1 + lax.broadcasted_iota(jnp.int32, (positions, width), 0)).astype(jnp.float32)
+    for mode in range(modes):
+        carry_rows[mode] = weights[mode : mode + 1] * jnp.exp(-rates[mode : mode + 1] * elapsed)
 
     def at_offset(piece, offset):
         return pl.ds(piece * rows + offset, SUBLANES, stride=run)
@@ -242,6 +245,24 @@
         def _():
             state_hop(distance).start()
 
+    entering = jnp.zeros((modes, width), jnp.float32)
+    for index in range(run_count):
+        entry_state[run_states(index)] = entering
+        if index + 1 < run_count:
+            entering = entering * run_decay + local_state[run_states(index)]
+    weight_all = weight_rows[...]
+    for piece in range(PIECES):
+        state = jnp.stack(
+            [
+                entry_state[pl.ds(mode * run_count + piece * SUBLANES, SUBLANES)]
+                for mode in range(modes)
+            ]
+        )
+        for offset in range(run):
+            state = state * decay_all + product[at_offset(piece, offset)][None]
+            conv[at_offset(piece, offset)] = jnp.sum(state * weight_all, axis=0)
+        conv[span(piece)] += skip[...] * product[span(piece)]
+
     carry[...] = jnp.zeros_like(carry)
     for distance in range(seq_count - 1, 0, -1):
 
@@ -257,43 +278,30 @@
             ).wait_recv()
             carry[...] = carry[...] * block_decay + states[block - distance]
 
-    entering = carry[...]
-    for index in range(run_count):
-        entry_state[run_states(index)] = entering
-        if index + 1 < run_count:
-            entering = entering * run_decay + local_state[run_states(index)]
-
-    weight_all = weight_rows[...]
-    for piece in range(PIECES):
-        state = jnp.stack(
-            [
-                entry_state[pl.ds(mode * run_count + piece * SUBLANES, SUBLANES)]
-                for mode in range(modes)
-            ]
-        )
-        for offset in range(run):
-            state = state * decay_all + product[at_offset(piece, offset)][None]
-            conv[at_offset(piece, offset)] = jnp.sum(state * weight_all, axis=0)
-        mixed = query[span(piece)] * (conv[span(piece)] + skip[...] * product[span(piece)])
-        mix_all[place, span(piece)] = mixed.astype(jnp.bfloat16)
+    for piece in range(PIECES):
+        gated = conv[span(piece)]
+        for mode in range(modes):
+            gated = gated + carry_rows[mode, span(piece)] * carry[mode : mode + 1]
+        mix_all[place, span(piece)] = (query[span(piece)] * gated).astype(jnp.bfloat16)
         send_own(mix_all, mix_send, mix_recv, piece, near + far)
 
+    pass_on(mix_all, mix_send, mix_recv)
+    for piece in range(PIECES):
+        finish_sends(tok_all, tok_send, tok_recv, piece, tok_ref)
+    for distance in range(1, seq_count):
+
+        @pl.when(block + distance < seq_count)
+        def _():
+            state_hop(distance).wait_send()
+
     wout_copy.wait()
-    pass_on(mix_all, mix_send, mix_recv)
     for piece in range(PIECES):
         out_ref[span(piece)] = jnp.dot(
             collect(mix_all, mix_send, mix_recv, piece),
             wout[...],
             preferred_element_type=jnp.float32,
         ).astype(out_ref.dtype)
-
-    finish_sends(tok_all, tok_send, tok_recv, tok_ref)
-    finish_sends(mix_all, mix_send, mix_recv)
-    for distance in range(1, seq_count):
-
-        @pl.when(block + distance < seq_count)
-        def _():
-            state_hop(distance).wait_send()
+        finish_sends(mix_all, mix_send, mix_recv, piece)
 
 
 def on_device(tokens, in_weight, out_weight, decay_rates, residues, skip_gain):
@@ -333,6 +341,7 @@
             pltpu.VMEM((modes, width), jnp.float32),
             pltpu.VMEM((modes, SUBLANES, width), jnp.float32),
             pltpu.VMEM((modes, SUBLANES, width), jnp.float32),
+            pltpu.VMEM((modes, positions, width), jnp.float32),
             pltpu.SemaphoreType.DMA((8,)),
             hops,
             hops,

time: 22.5 us -> 22.4 us (level)
  no operation moved by 1% of the time
where the time goes in v4:
time: 22.4 us; the launch traced here: 22.2 us
  Pallas kernels  21.6 us (96%)
  local copies, waits for them, and re-layouts  0.63 us (3%)
    pallas_call x1, Pallas kernels, on_device(): pl.pallas_call(functools.partial(block_kernel, chan_count, seq_count), ou...  21.6 us
    unnamed x1, local copies, waits for them, and re-layouts  0.63 us

profile of v4, /device:TPU:4, one launch (start us, length us, event | category | flops | bytes accessed | tf_op | source)
XLA Modules:
  0.0 22.2 jit_solution(2897757436821400477)
XLA Ops:
  0.0 21.6 %hyena_block.1 = bf16[256,128]{1,0:T(8,128)(2,1)S(1)} custom-call(bf16[256,128]{1,0:T(8,128)(2,1)} %tok_ref.1, bf16[3,512,128]{2,1,0:T(8,128)(2,1)} %win_ref.1, bf16[512,128]{1,0:T(8,128)(2,1)} %wout_ref.1, f32[16,128]{1,0:T(8,128)} %rate_ref.1, f32[16,128]{1,0:T(8,128)} %res_ref.1, f32[1,128]{1,0:T(1,128)} %bitcast.1), custom_call_target="tpu_custom_call" | custom-call | tf_op jit(solution)/shard_map/hyena_block/pallas_call | solution.py:322
  21.6 0.6 %copy.8 = bf16[256,128]{1,0:T(8,128)(2,1)} copy(bf16[256,128]{1,0:T(8,128)(2,1)S(1)} %hyena_block.1) | data formatting | bytes 131072

commit v5 on v4

--- a/solution.py
+++ b/solution.py
@@ -63,11 +63,9 @@
     for distance in range(1, chan_count):
         greet("chan", lax.rem(place + distance, chan_count))
 
-    for distance in range(1, seq_count):
-
-        @pl.when(block >= distance)
-        def _():
-            greet("seq", block - distance)
+    @pl.loop(1, block + 1)
+    def _(distance):
+        greet("seq", block - distance)
 
     pl.semaphore_wait(barrier, seq_count - 1 - block + chan_count - 1)
 
@@ -201,8 +199,12 @@
 
     pass_on(tok_all, tok_send, tok_recv)
     elapsed = (1 + lax.broadcasted_iota(jnp.int32, (positions, width), 0)).astype(jnp.float32)
-    for mode in range(modes):
-        carry_rows[mode] = weights[mode : mode + 1] * jnp.exp(-rates[mode : mode + 1] * elapsed)
+
+    @pl.loop(0, modes)
+    def _(mode):
+        mode_rate = rate[pl.ds(mode, 1)]
+        mode_weight = res[pl.ds(mode, 1)] * jnp.sqrt(2.0 * mode_rate)
+        carry_rows[mode] = mode_weight * jnp.exp(-mode_rate * elapsed)
 
     def at_offset(piece, offset):
         return pl.ds(piece * rows + offset, SUBLANES, stride=run)
@@ -215,9 +217,13 @@
         ).astype(jnp.bfloat16).astype(jnp.float32)
         query[span(piece)] = projected[:, :width]
         product[span(piece)] = projected[:, width : 2 * width] * projected[:, 2 * width :]
-        state = jnp.zeros((modes, SUBLANES, width), jnp.float32)
-        for offset in range(run):
-            state = state * decay_all + product[at_offset(piece, offset)][None]
+        state = lax.fori_loop(
+            0,
+            run,
+            lambda offset, state: state * decay_all + product[at_offset(piece, offset)][None],
+            jnp.zeros((modes, SUBLANES, width), jnp.float32),
+            unroll=4,
+        )
         for mode in range(modes):
             local_state[pl.ds(mode * run_count + piece * SUBLANES, SUBLANES)] = state[mode]
 
@@ -239,11 +245,9 @@
             device_id_type=MESH,
         )
 
-    for distance in range(1, seq_count):
-
-        @pl.when(block + distance < seq_count)
-        def _():
-            state_hop(distance).start()
+    @pl.loop(1, seq_count - block)
+    def _(distance):
+        state_hop(distance).start()
 
     entering = jnp.zeros((modes, width), jnp.float32)
     for index in range(run_count):
@@ -251,48 +255,53 @@
         if index + 1 < run_count:
             entering = entering * run_decay + local_state[run_states(index)]
     weight_all = weight_rows[...]
-    for piece in range(PIECES):
-        state = jnp.stack(
-            [
-                entry_state[pl.ds(mode * run_count + piece * SUBLANES, SUBLANES)]
-                for mode in range(modes)
-            ]
-        )
-        for offset in range(run):
+
+    @pl.loop(0, PIECES)
+    def _(piece):
+        def advance(offset, state):
             state = state * decay_all + product[at_offset(piece, offset)][None]
             conv[at_offset(piece, offset)] = jnp.sum(state * weight_all, axis=0)
-        conv[span(piece)] += skip[...] * product[span(piece)]
+            return state
+
+        first = [
+            entry_state[pl.ds(pl.multiple_of(mode * run_count + piece * SUBLANES, SUBLANES), SUBLANES)]
+            for mode in range(modes)
+        ]
+        lax.fori_loop(0, run, advance, jnp.stack(first), unroll=2)
+
+    conv[...] += skip[...] * product[...]
 
     carry[...] = jnp.zeros_like(carry)
-    for distance in range(seq_count - 1, 0, -1):
-
-        @pl.when(block >= distance)
-        def _():
-            pltpu.make_async_remote_copy(
-                src_ref=states.at[block - distance],
-                dst_ref=states.at[block - distance],
-                send_sem=state_send.at[distance],
-                recv_sem=state_recv.at[distance],
-                device_id={"seq": block - distance},
-                device_id_type=MESH,
-            ).wait_recv()
-            carry[...] = carry[...] * block_decay + states[block - distance]
+
+    @pl.loop(0, block)
+    def _(source):
+        pltpu.make_async_remote_copy(
+            src_ref=states.at[source],
+            dst_ref=states.at[source],
+            send_sem=state_send.at[block - source],
+            recv_sem=state_recv.at[block - source],
+            device_id={"seq": source},
+            device_id_type=MESH,
+        ).wait_recv()
+        carry[...] = carry[...] * block_decay + states[source]
 
     for piece in range(PIECES):
-        gated = conv[span(piece)]
-        for mode in range(modes):
-            gated = gated + carry_rows[mode, span(piece)] * carry[mode : mode + 1]
+        gated = lax.fori_loop(
+            0,
+            modes,
+            lambda mode, gated: gated + carry_rows[mode, span(piece)] * carry[pl.ds(mode, 1)],
+            conv[span(piece)],
+            unroll=2,
+        )
         mix_all[place, span(piece)] = (query[span(piece)] * gated).astype(jnp.bfloat16)
         send_own(mix_all, mix_send, mix_recv, piece, near + far)
 
     pass_on(mix_all, mix_send, mix_recv)
     for piece in range(PIECES):
         finish_sends(tok_all, tok_send, tok_recv, piece, tok_ref)
-    for distance in range(1, seq_count):
-
-        @pl.when(block + distance < seq_count)
-        def _():
-            state_hop(distance).wait_send()
+    @pl.loop(1, seq_count - block)
+    def _(distance):
+        state_hop(distance).wait_send()
 
     wout_copy.wait()
     for piece in range(PIECES):

time: 22.4 us -> 22.4 us (level)
  no operation moved by 1% of the time
where the time goes in v5:
time: 22.4 us; the launch traced here: 22.3 us
  Pallas kernels  21.7 us (97%)
  local copies, waits for them, and re-layouts  0.63 us (3%)
    pallas_call x1, Pallas kernels, on_device(): pl.pallas_call(functools.partial(block_kernel, chan_count, seq_count), ou...  21.7 us
    unnamed x1, local copies, waits for them, and re-layouts  0.63 us

profile of v5, /device:TPU:4, one launch (start us, length us, event | category | flops | bytes accessed | tf_op | source)
XLA Modules:
  0.0 22.3 jit_solution(17312935187249252449)
XLA Ops:
  0.0 21.7 %hyena_block.1 = bf16[256,128]{1,0:T(8,128)(2,1)S(1)} custom-call(bf16[256,128]{1,0:T(8,128)(2,1)} %tok_ref.1, bf16[3,512,128]{2,1,0:T(8,128)(2,1)} %win_ref.1, bf16[512,128]{1,0:T(8,128)(2,1)} %wout_ref.1, f32[16,128]{1,0:T(8,128)} %rate_ref.1, f32[16,128]{1,0:T(8,128)} %res_ref.1, f32[1,128]{1,0:T(1,128)} %bitcast.1), custom_call_target="tpu_custom_call" | custom-call | tf_op jit(solution)/shard_map/hyena_block/pallas_call | solution.py:331
  21.7 0.6 %copy.8 = bf16[256,128]{1,0:T(8,128)(2,1)} copy(bf16[256,128]{1,0:T(8,128)(2,1)S(1)} %hyena_block.1) | data formatting | bytes 131072

commit v6 on v5

--- a/solution.py
+++ b/solution.py
@@ -90,11 +90,10 @@
     def goes_direct(distance):
         target = lax.rem(place + distance, chan_count)
         direct = None
-        for step, relay, end in relays:
-            if distance == 2 * step % chan_count:
-                owner = (end - 2 * step) % chan_count
-                here = jnp.logical_not(jnp.logical_and(place == owner, target == end))
-                direct = here if direct is None else jnp.logical_and(direct, here)
+        for step, _, end in relays:
+            owner = (end - 2 * step) % chan_count
+            here = jnp.logical_not(jnp.logical_and(place == owner, target == end))
+            direct = here if direct is None else jnp.logical_and(direct, here)
         return direct
 
     def when(condition, action):
@@ -106,8 +105,9 @@
     near = sorted({1, chan_count - 1} - {0})
     far = [distance for distance in range(2, chan_count - 1)]
 
-    def send_own(buffer, sends, recvs, piece, distances, source=None):
-        for distance in distances:
+    def send_own(buffer, sends, recvs, piece, source=None):
+        for order in range(1, chan_count):
+            distance = jnp.where(place < chan_count // 2, chan_count - order, order)
             copy = hop(buffer, sends, recvs, distance, piece, source)
             when(goes_direct(distance), copy.start)
 
@@ -157,28 +157,21 @@
             copy = relay_hop(buffer, sends, recvs, piece, step, end)
             pl.when(place == relay)(copy.wait_send)
 
-    for distances in (near, far):
-        for piece in range(PIECES):
-            send_own(tok_all, tok_send, tok_recv, piece, distances, tok_ref)
+    for piece in range(PIECES):
+        send_own(tok_all, tok_send, tok_recv, piece, tok_ref)
 
     own_tokens = pltpu.make_async_copy(tok_ref, tok_all.at[place], local_sem.at[0])
     own_tokens.start()
-    win_copies = [
-        pltpu.make_async_copy(
-            win_ref.at[index], win.at[:, pl.ds(index * width, width)], local_sem.at[1 + index]
-        )
-        for index in range(3)
-    ]
-    for copy in win_copies:
-        copy.start()
+    win_copy = pltpu.make_async_copy(win_ref, win, local_sem.at[1])
+    win_copy.start()
     small_copies = [
-        pltpu.make_async_copy(rate_ref, rate, local_sem.at[4]),
-        pltpu.make_async_copy(res_ref, res, local_sem.at[5]),
-        pltpu.make_async_copy(skip_ref, skip, local_sem.at[6]),
+        pltpu.make_async_copy(rate_ref, rate, local_sem.at[2]),
+        pltpu.make_async_copy(res_ref, res, local_sem.at[3]),
+        pltpu.make_async_copy(skip_ref, skip, local_sem.at[4]),
     ]
     for copy in small_copies:
         copy.start()
-    wout_copy = pltpu.make_async_copy(wout_ref, wout, local_sem.at[7])
+    wout_copy = pltpu.make_async_copy(wout_ref, wout, local_sem.at[5])
     wout_copy.start()
 
     for copy in small_copies:
@@ -194,8 +187,7 @@
     decay_all = decay_rows[...]
 
     own_tokens.wait()
-    for copy in win_copies:
-        copy.wait()
+    win_copy.wait()
 
     pass_on(tok_all, tok_send, tok_recv)
     elapsed = (1 + lax.broadcasted_iota(jnp.int32, (positions, width), 0)).astype(jnp.float32)
@@ -212,7 +204,7 @@
     for piece in range(PIECES):
         projected = jnp.dot(
             collect(tok_all, tok_send, tok_recv, piece),
-            win[...],
+            jnp.concatenate([win[index] for index in range(3)], axis=1),
             preferred_element_type=jnp.float32,
         ).astype(jnp.bfloat16).astype(jnp.float32)
         query[span(piece)] = projected[:, :width]
@@ -294,7 +286,7 @@
             unroll=2,
         )
         mix_all[place, span(piece)] = (query[span(piece)] * gated).astype(jnp.bfloat16)
-        send_own(mix_all, mix_send, mix_recv, piece, near + far)
+        send_own(mix_all, mix_send, mix_recv, piece)
 
     pass_on(mix_all, mix_send, mix_recv)
     for piece in range(PIECES):
@@ -336,7 +328,7 @@
         scratch_shapes=[
             pltpu.VMEM((chan_count, positions, width), jnp.bfloat16),
             pltpu.VMEM((chan_count, positions, width), jnp.bfloat16),
-            pltpu.VMEM((channels, 3 * width), jnp.bfloat16),
+            pltpu.VMEM((3, channels, width), jnp.bfloat16),
             pltpu.VMEM((channels, width), jnp.bfloat16),
             pltpu.VMEM((modes, width), jnp.float32),
             pltpu.VMEM((modes, width), jnp.float32),
@@ -351,7 +343,7 @@
             pltpu.VMEM((modes, SUBLANES, width), jnp.float32),
             pltpu.VMEM((modes, SUBLANES, width), jnp.float32),
             pltpu.VMEM((modes, positions, width), jnp.float32),
-            pltpu.SemaphoreType.DMA((8,)),
+            pltpu.SemaphoreType.DMA((6,)),
             hops,
             hops,
             hops,

time: 22.4 us -> 22.7 us (1.013)
    pallas_call x1, Pallas kernels: 21.7 us -> 21.9 us  [on_device(): pl.pallas_call(functools.partial(block_kernel, chan_count, seq_count), ou...]
where the time goes in v6:
time: 22.7 us; the launch traced here: 22.5 us
  Pallas kernels  21.9 us (96%)
  local copies, waits for them, and re-layouts  0.63 us (3%)
    pallas_call x1, Pallas kernels, on_device(): pl.pallas_call(functools.partial(block_kernel, chan_count, seq_count), ou...  21.9 us
    unnamed x1, local copies, waits for them, and re-layouts  0.63 us

profile of v6, /device:TPU:4, one launch (start us, length us, event | category | flops | bytes accessed | tf_op | source)
XLA Modules:
  0.0 22.5 jit_solution(15310757793657632994)
XLA Ops:
  0.0 21.9 %hyena_block.1 = bf16[256,128]{1,0:T(8,128)(2,1)S(1)} custom-call(bf16[256,128]{1,0:T(8,128)(2,1)} %tok_ref.1, bf16[3,512,128]{2,1,0:T(8,128)(2,1)} %win_ref.1, bf16[512,128]{1,0:T(8,128)(2,1)} %wout_ref.1, f32[16,128]{1,0:T(8,128)} %rate_ref.1, f32[16,128]{1,0:T(8,128)} %res_ref.1, f32[1,128]{1,0:T(1,128)} %bitcast.1), custom_call_target="tpu_custom_call" | custom-call | tf_op jit(solution)/shard_map/hyena_block/pallas_call | solution.py:323
  21.9 0.6 %copy.8 = bf16[256,128]{1,0:T(8,128)(2,1)} copy(bf16[256,128]{1,0:T(8,128)(2,1)S(1)} %hyena_block.1) | data formatting | bytes 131072

commit v7 on v5

--- a/solution.py
+++ b/solution.py
@@ -67,6 +67,20 @@
     def _(distance):
         greet("seq", block - distance)
 
+    own_tokens = pltpu.make_async_copy(tok_ref, tok_all.at[place], local_sem.at[0])
+    own_tokens.start()
+    win_copy = pltpu.make_async_copy(win_ref, win, local_sem.at[1])
+    win_copy.start()
+    small_copies = [
+        pltpu.make_async_copy(rate_ref, rate, local_sem.at[2]),
+        pltpu.make_async_copy(res_ref, res, local_sem.at[3]),
+        pltpu.make_async_copy(skip_ref, skip, local_sem.at[4]),
+    ]
+    for copy in small_copies:
+        copy.start()
+    wout_copy = pltpu.make_async_copy(wout_ref, wout, local_sem.at[5])
+    wout_copy.start()
+
     pl.semaphore_wait(barrier, seq_count - 1 - block + chan_count - 1)
 
     def span(piece):
@@ -90,7 +104,7 @@
     def goes_direct(distance):
         target = lax.rem(place + distance, chan_count)
         direct = None
-        for step, relay, end in relays:
+        for step, _, end in relays:
             if distance == 2 * step % chan_count:
                 owner = (end - 2 * step) % chan_count
                 here = jnp.logical_not(jnp.logical_and(place == owner, target == end))
@@ -160,26 +174,6 @@
     for distances in (near, far):
         for piece in range(PIECES):
             send_own(tok_all, tok_send, tok_recv, piece, distances, tok_ref)
-
-    own_tokens = pltpu.make_async_copy(tok_ref, tok_all.at[place], local_sem.at[0])
-    own_tokens.start()
-    win_copies = [
-        pltpu.make_async_copy(
-            win_ref.at[index], win.at[:, pl.ds(index * width, width)], local_sem.at[1 + index]
-        )
-        for index in range(3)
-    ]
-    for copy in win_copies:
-        copy.start()
-    small_copies = [
-        pltpu.make_async_copy(rate_ref, rate, local_sem.at[4]),
-        pltpu.make_async_copy(res_ref, res, local_sem.at[5]),
-        pltpu.make_async_copy(skip_ref, skip, local_sem.at[6]),
-    ]
-    for copy in small_copies:
-        copy.start()
-    wout_copy = pltpu.make_async_copy(wout_ref, wout, local_sem.at[7])
-    wout_copy.start()
 
     for copy in small_copies:
         copy.wait()
@@ -194,8 +188,7 @@
     decay_all = decay_rows[...]
 
     own_tokens.wait()
-    for copy in win_copies:
-        copy.wait()
+    win_copy.wait()
 
     pass_on(tok_all, tok_send, tok_recv)
     elapsed = (1 + lax.broadcasted_iota(jnp.int32, (positions, width), 0)).astype(jnp.float32)
@@ -212,7 +205,7 @@
     for piece in range(PIECES):
         projected = jnp.dot(
             collect(tok_all, tok_send, tok_recv, piece),
-            win[...],
+            jnp.concatenate([win[index] for index in range(3)], axis=1),
             preferred_element_type=jnp.float32,
         ).astype(jnp.bfloat16).astype(jnp.float32)
         query[span(piece)] = projected[:, :width]
@@ -336,7 +329,7 @@
         scratch_shapes=[
             pltpu.VMEM((chan_count, positions, width), jnp.bfloat16),
             pltpu.VMEM((chan_count, positions, width), jnp.bfloat16),
-            pltpu.VMEM((channels, 3 * width), jnp.bfloat16),
+            pltpu.VMEM((3, channels, width), jnp.bfloat16),
             pltpu.VMEM((channels, width), jnp.bfloat16),
             pltpu.VMEM((modes, width), jnp.float32),
             pltpu.VMEM((modes, width), jnp.float32),
@@ -351,7 +344,7 @@
             pltpu.VMEM((modes, SUBLANES, width), jnp.float32),
             pltpu.VMEM((modes, SUBLANES, width), jnp.float32),
             pltpu.VMEM((modes, positions, width), jnp.float32),
-            pltpu.SemaphoreType.DMA((8,)),
+            pltpu.SemaphoreType.DMA((6,)),
             hops,
             hops,
             hops,

time: 22.4 us -> 22.4 us (level)
  no operation moved by 1% of the time
where the time goes in v7:
time: 22.4 us; the launch traced here: 22.3 us
  Pallas kernels  21.6 us (96%)
  local copies, waits for them, and re-layouts  0.63 us (3%)
    pallas_call x1, Pallas kernels, on_device(): pl.pallas_call(functools.partial(block_kernel, chan_count, seq_count), ou...  21.6 us
    unnamed x1, local copies, waits for them, and re-layouts  0.63 us

profile of v7, /device:TPU:4, one launch (start us, length us, event | category | flops | bytes accessed | tf_op | source)
XLA Modules:
  0.0 22.3 jit_solution(9650203006180331003)
XLA Ops:
  0.0 21.6 %hyena_block.1 = bf16[256,128]{1,0:T(8,128)(2,1)S(1)} custom-call(bf16[256,128]{1,0:T(8,128)(2,1)} %tok_ref.1, bf16[3,512,128]{2,1,0:T(8,128)(2,1)} %win_ref.1, bf16[512,128]{1,0:T(8,128)(2,1)} %wout_ref.1, f32[16,128]{1,0:T(8,128)} %rate_ref.1, f32[16,128]{1,0:T(8,128)} %res_ref.1, f32[1,128]{1,0:T(1,128)} %bitcast.1), custom_call_target="tpu_custom_call" | custom-call | tf_op jit(solution)/shard_map/hyena_block/pallas_call | solution.py:324
  21.6 0.6 %copy.8 = bf16[256,128]{1,0:T(8,128)(2,1)} copy(bf16[256,128]{1,0:T(8,128)(2,1)S(1)} %hyena_block.1) | data formatting | bytes 131072

commit v8 on v7

--- a/solution.py
+++ b/solution.py
@@ -239,8 +239,8 @@
         )
 
     @pl.loop(1, seq_count - block)
-    def _(distance):
-        state_hop(distance).start()
+    def _(order):
+        state_hop(seq_count - block - order).start()
 
     entering = jnp.zeros((modes, width), jnp.float32)
     for index in range(run_count):

time: 22.4 us -> 22.5 us (level)
  no operation moved by 1% of the time
where the time goes in v8:
time: 22.5 us; the launch traced here: 22.3 us
  Pallas kernels  21.7 us (96%)
  local copies, waits for them, and re-layouts  0.63 us (3%)
    pallas_call x1, Pallas kernels, on_device(): pl.pallas_call(functools.partial(block_kernel, chan_count, seq_count), ou...  21.7 us
    unnamed x1, local copies, waits for them, and re-layouts  0.63 us

profile of v8, /device:TPU:4, one launch (start us, length us, event | category | flops | bytes accessed | tf_op | source)
XLA Modules:
  0.0 22.3 jit_solution(13163651763492857995)
XLA Ops:
  0.0 21.7 %hyena_block.1 = bf16[256,128]{1,0:T(8,128)(2,1)S(1)} custom-call(bf16[256,128]{1,0:T(8,128)(2,1)} %tok_ref.1, bf16[3,512,128]{2,1,0:T(8,128)(2,1)} %win_ref.1, bf16[512,128]{1,0:T(8,128)(2,1)} %wout_ref.1, f32[16,128]{1,0:T(8,128)} %rate_ref.1, f32[16,128]{1,0:T(8,128)} %res_ref.1, f32[1,128]{1,0:T(1,128)} %bitcast.1), custom_call_target="tpu_custom_call" | custom-call | tf_op jit(solution)/shard_map/hyena_block/pallas_call | solution.py:324
  21.7 0.6 %copy.8 = bf16[256,128]{1,0:T(8,128)(2,1)} copy(bf16[256,128]{1,0:T(8,128)(2,1)S(1)} %hyena_block.1) | data formatting | bytes 131072

commit v9 on v7

--- a/solution.py
+++ b/solution.py
@@ -202,6 +202,10 @@
     def at_offset(piece, offset):
         return pl.ds(piece * rows + offset, SUBLANES, stride=run)
 
+    def run_states(index):
+        return pl.ds(index, modes, stride=run_count)
+
+    total = jnp.zeros((modes, width), jnp.float32)
     for piece in range(PIECES):
         projected = jnp.dot(
             collect(tok_all, tok_send, tok_recv, piece),
@@ -219,13 +223,10 @@
         )
         for mode in range(modes):
             local_state[pl.ds(mode * run_count + piece * SUBLANES, SUBLANES)] = state[mode]
-
-    def run_states(index):
-        return pl.ds(index, modes, stride=run_count)
-
-    total = local_state[run_states(0)]
-    for index in range(1, run_count):
-        total = total * run_decay + local_state[run_states(index)]
+        for index in range(piece * SUBLANES, (piece + 1) * SUBLANES):
+            entry_state[run_states(index)] = total
+            total = total * run_decay + local_state[run_states(index)]
+
     states[block] = total
 
     def state_hop(distance):
@@ -242,11 +243,6 @@
     def _(distance):
         state_hop(distance).start()
 
-    entering = jnp.zeros((modes, width), jnp.float32)
-    for index in range(run_count):
-        entry_state[run_states(index)] = entering
-        if index + 1 < run_count:
-            entering = entering * run_decay + local_state[run_states(index)]
     weight_all = weight_rows[...]
 
     @pl.loop(0, PIECES)

time: 22.4 us -> 22.4 us (level)
  no operation moved by 1% of the time
where the time goes in v9:
time: 22.4 us; the launch traced here: 22.3 us
  Pallas kernels  21.6 us (96%)
  local copies, waits for them, and re-layouts  0.63 us (3%)
    pallas_call x1, Pallas kernels, on_device(): pl.pallas_call(functools.partial(block_kernel, chan_count, seq_count), ou...  21.6 us
    unnamed x1, local copies, waits for them, and re-layouts  0.63 us

profile of v9, /device:TPU:4, one launch (start us, length us, event | category | flops | bytes accessed | tf_op | source)
XLA Modules:
  0.0 22.3 jit_solution(10026336035033740167)
XLA Ops:
  0.0 21.6 %hyena_block.1 = bf16[256,128]{1,0:T(8,128)(2,1)S(1)} custom-call(bf16[256,128]{1,0:T(8,128)(2,1)} %tok_ref.1, bf16[3,512,128]{2,1,0:T(8,128)(2,1)} %win_ref.1, bf16[512,128]{1,0:T(8,128)(2,1)} %wout_ref.1, f32[16,128]{1,0:T(8,128)} %rate_ref.1, f32[16,128]{1,0:T(8,128)} %res_ref.1, f32[1,128]{1,0:T(1,128)} %bitcast.1), custom_call_target="tpu_custom_call" | custom-call | tf_op jit(solution)/shard_map/hyena_block/pallas_call | solution.py:320
  21.7 0.6 %copy.8 = bf16[256,128]{1,0:T(8,128)(2,1)} copy(bf16[256,128]{1,0:T(8,128)(2,1)S(1)} %hyena_block.1) | data formatting | bytes 131072
